TPU v7x, 32 devices: a whole 2x2x4 slice. The times are simulated.
32 devices in a mesh: row: 8 (over z, x), col: 4 (over y, core).
Axes of the slice: x: 2, y: 2, z: 4, core: 2. Of those that a mesh axis runs over, the one named last changes fastest.
Arguments:
- stereo_neuron_outputs: bfloat16 [2, 64, 64, 512], P(None, 'row', None, 'col'), may hold values from -6 to 6
- filter_tap_coefficients: bfloat16 [3, 3, 3, 64, 64], replicated, may hold values from -0.25 to 0.25
- filter_stack_intercepts: float32 [3, 64], replicated, may hold values from -3 to 3
- reference_picture_present: int32 [64, 512], P('row', 'col'), may hold values 0 or 1
- tile_shift_amounts: int32 [8, 4], P('row', 'col'), may hold values from 0 to 256, as said below
- smoothness_charges: int32 [2], replicated, may hold values from 4 to 96, as said below
Outputs:
- aggregated: float32 [64, 512, 128], P('row', 'col')
Inputs may be any that keep to these rules, and one draw needn't show every extreme that they name: `tile_shift_amounts`: every tile's offset is a whole number of 0 to 256; some tile has exactly 256. smoothness_charges[0] lies in 4 to 16; smoothness_charges[1] is 96.
All inputs are finite; a program needn't handle non-finite values. No bound on the sum of `reference_picture_present` on one device may be relied on, other than what follows from the above.
Results may differ from a plain program's by a relative error of at most 0.006.
Values may be sent and summed in bfloat16 or wider, within the bound.
No kernel may reach another device: no remote copies, remote signals or barrier semaphores. Data moves between devices by JAX's collectives and lax.ppermute only.
A program may use at most 64 MiB of HBM per device.

v0:
```python
import functools

import jax
import jax.numpy as jnp
from jax import lax
from jax.experimental import pallas as pl
from jax.experimental.pallas import tpu as pltpu
from jax.sharding import PartitionSpec as P

DISPARITIES = 128
OFF_MOST = 256
SUB = 8
REGS = DISPARITIES // SUB
MEBI = 1024 * 1024


def lane_to_disparity(lane):
    return (lane % SUB) * REGS + lane // SUB


def disparity_to_lane(disparity):
    return (disparity % REGS) * SUB + disparity // REGS


def advance(state, cost, p1, p2):
    lanes = state[0].shape[1]
    row = lax.broadcasted_iota(jnp.int32, (SUB, lanes), 0)
    below = jnp.where(row == 0, jnp.inf, pltpu.roll(state[-1], 1, 0))
    above = jnp.where(row == SUB - 1, jnp.inf, pltpu.roll(state[0], SUB - 1, 0))
    least = list(state)
    while len(least) > 1:
        least = [jnp.minimum(a, b) for a, b in zip(least[::2], least[1::2])]
    least = least[0]
    turned = [least] + [pltpu.roll(least, turn, 0) for turn in range(1, SUB)]
    while len(turned) > 1:
        turned = [jnp.minimum(a, b) for a, b in zip(turned[::2], turned[1::2])]
    least = turned[0]
    lower = [below] + state[:-1]
    upper = state[1:] + [above]
    fresh = []
    for s, l, u, c in zip(state, lower, upper, cost):
        t = jnp.minimum(s, jnp.minimum(l, u) + p1)
        fresh.append(c + jnp.minimum(t - least, p2))
    return fresh


def charges(charge_ref):
    return (
        charge_ref[0].astype(jnp.float32) * (1.0 / 64.0),
        charge_ref[1].astype(jnp.float32) * (1.0 / 64.0),
    )


def registers(array):
    return [array[SUB * v : SUB * (v + 1)] for v in range(REGS)]


def band_kernel(masks, place_ref, filter_ref, bias_ref, *refs):
    parts = len(masks)
    tile_refs, edge_refs, refs = refs[:parts], refs[parts : 2 * parts], refs[2 * parts :]
    cost_ref, own_ref, maps_a, maps_b, left_unit, right_unit, present, shifts = refs
    _, channels, width = tile_refs[0].shape
    layers = filter_ref.shape[0]
    rows = own_ref.shape[0]
    cols = parts * width
    high = rows + 2 * layers
    first_row = place_ref[0] * rows
    rows_total = place_ref[1] * rows
    own = place_ref[2]
    lead = (OFF_MOST + 2 * width - 1) // width * width

    for mask, edge_ref in zip(masks, edge_refs):
        member = own ^ mask
        extra = edge_ref[4 * layers].astype(jnp.float32)
        present[:, pl.ds(pl.multiple_of(member * width, width), width)] = extra[0:16]
        shifts[member] = extra[16:24]
    right_unit[:, 0:lead] = jnp.zeros((rows * channels, lead), jnp.bfloat16)
    right_unit[:, lead + cols :] = jnp.zeros((rows * channels, width), jnp.bfloat16)

    column = lax.broadcasted_iota(jnp.int32, (1, cols), 1)
    for image in range(2):

        for mask, tile_ref, edge_ref in zip(masks, tile_refs, edge_refs):
            there = pl.ds(pl.multiple_of((own ^ mask) * width, width), width)
            for row in range(high):
                if row < layers:
                    value = edge_ref[image * layers + row]
                elif row < layers + rows:
                    value = tile_ref[image * rows + row - layers]
                else:
                    value = edge_ref[(2 + image) * layers + row - layers - rows]
                maps_a[row * channels : (row + 1) * channels, there] = value

        for layer in range(layers):
            source, target = (maps_a, maps_b) if layer % 2 == 0 else (maps_b, maps_a)
            margin = layers - 1 - layer

            steps = rows + 2 * margin

            @pl.loop(0, steps, unroll=max(k for k in range(1, 6) if steps % k == 0))
            def _(row):
                start = pl.multiple_of(row * channels, channels)
                window = source[pl.ds(start, 3 * channels), :]
                taps = jnp.dot(filter_ref[layer], window, preferred_element_type=jnp.float32)
                before = pltpu.roll(taps[:channels], 1, 1)
                after = pltpu.roll(taps[2 * channels :], cols - 1, 1)
                z = taps[channels : 2 * channels] + jnp.where(column == 0, 0.0, before)
                z = z + jnp.where(column == cols - 1, 0.0, after) + bias_ref[layer]
                if layer < layers - 1:
                    there = first_row - margin + row
                    inside = jnp.logical_and(there >= 0, there < rows_total)
                    z = jnp.maximum(z, 0.0) * jnp.where(inside, 1.0, 0.0)
                    target[pl.ds(start, channels), :] = z.astype(jnp.bfloat16)
                else:
                    scale = lax.rsqrt(jnp.sum(z * z, axis=0, keepdims=True) + 1e-06)
                    unit = (z * scale).astype(jnp.bfloat16)
                    if image == 0:
                        seen = present[pl.ds(row, 1), :]
                        unit = jnp.where(seen > 0.5, unit.astype(jnp.float32), 0.0)
                        left_unit[pl.ds(start, channels), :] = unit.astype(jnp.bfloat16)
                    else:
                        right_unit[pl.ds(start, channels), lead : lead + cols] = unit

    lane = lax.broadcasted_iota(jnp.int32, (width, DISPARITIES), 1)
    place = lax.broadcasted_iota(jnp.int32, (width, DISPARITIES), 0)

    @pl.loop(0, parts)
    def _(p):
        shift = jnp.max(shifts[p]).astype(jnp.int32)
        base = p * width - shift + lead
        block = base // width
        ahead = place + (base - block * width)
        index = (ahead - lane_to_disparity(lane)) & (DISPARITIES - 1)
        start = pl.multiple_of((block - 1) * width, width)
        here = pl.multiple_of(p * width, width)

        def tile_costs(mine):
            for y in range(rows):
                left = left_unit[y * channels : (y + 1) * channels, pl.ds(here, width)]
                right = right_unit[y * channels : (y + 1) * channels, pl.ds(start, 3 * width)]
                product = lax.dot_general(
                    left, right, (((0,), (0,)), ((), ())), preferred_element_type=jnp.float32
                )
                chosen = jnp.where(lane <= ahead, product[:, width : 2 * width], product[:, :width])
                chosen = jnp.where(lane <= ahead - width, product[:, 2 * width :], chosen)
                chosen = jnp.take_along_axis(chosen, index, axis=1, mode="promise_in_bounds")
                chosen = 1.0 - chosen
                cost_ref[pl.ds(here, width), y, :] = chosen
                if mine:
                    own_ref[y] = chosen.T.astype(jnp.bfloat16)

        pl.when(p == own)(functools.partial(tile_costs, True))
        pl.when(p != own)(functools.partial(tile_costs, False))


def across_kernel(second, place_ref, charge_ref, cost_ref, *refs):
    kept_ref, last_ref = refs[-2:]
    cols = cost_ref.shape[0]
    width, rows, _ = kept_ref.shape
    parts = cols // width
    own = place_ref[2]
    p1, p2 = charges(charge_ref)

    def segment(p, state):
        first_col = p * width
        last_col = cols - 1 - p * width

        def run(keep_right, keep_left, state):
            def body(i, state):
                pair = [cost_ref[first_col + i], cost_ref[last_col - i]]
                cost = jnp.concatenate(pair, axis=0).T
                fresh = advance(list(state), registers(cost), p1, p2)
                if keep_right or keep_left:
                    back = jnp.concatenate(fresh, axis=0).T
                if keep_right:
                    kept_ref[i] = back[0:rows]
                if keep_left:
                    kept_ref[width - 1 - i] = back[rows : 2 * rows]
                return tuple(fresh)

            return lax.fori_loop(0, width, body, state, unroll=16)

        choice = jnp.where(p == own, 1, 0) + jnp.where(parts - 1 - p == own, 2, 0)
        return lax.switch(
            choice,
            [functools.partial(run, k == 1, k == 2) for k in range(3)],
            state,
        )

    if second:
        state = tuple(registers(refs[0][...]))
        span = (parts // 2, parts)
    else:
        state = tuple(jnp.zeros((SUB, 2 * rows), jnp.float32) for _ in range(REGS))
        span = (0, parts // 2)
    last_ref[...] = jnp.concatenate(lax.fori_loop(*span, segment, state), axis=0)


def down_or_up(forward, first_own, cost_ref, state, p1, p2, keep):
    group, rows = cost_ref.shape[:2]

    def block(b, state):
        member = jnp.where(forward, b, group - 1 - b)

        def run(kept, state):
            for i in range(rows):
                inner = jnp.where(forward, i, rows - 1 - i)
                cost = cost_ref[member, inner].astype(jnp.float32)
                state = advance(list(state), registers(cost), p1, p2)
                if kept:
                    keep(inner, jnp.concatenate(state, axis=0))
            return tuple(state)

        return lax.cond(
            member == first_own,
            functools.partial(run, True),
            functools.partial(run, False),
            state,
        )

    return lax.fori_loop(0, group, block, state)


def first_vertical_kernel(place_ref, charge_ref, *refs):
    *block_refs, kept_ref, last_ref, cost_ref = refs
    p1, p2 = charges(charge_ref)
    group, _, _, width = cost_ref.shape
    for k, block_ref in enumerate(block_refs):
        cost_ref[lax.rem(place_ref[4] + group - k, group)] = block_ref[...]
    state = tuple(jnp.zeros((SUB, width), jnp.float32) for _ in range(REGS))

    def keep(row, value):
        kept_ref[row] = value

    final = down_or_up(place_ref[3] == 0, place_ref[4], cost_ref, state, p1, p2, keep)
    last_ref[...] = jnp.concatenate(final, axis=0).astype(jnp.bfloat16)


def second_vertical_kernel(place_ref, charge_ref, *refs):
    *block_refs, kept_ref, came_ref, early_ref, late_ref, out_ref, total, cost_ref = refs
    p1, p2 = charges(charge_ref)
    group = cost_ref.shape[0]
    for k, block_ref in enumerate(block_refs):
        cost_ref[lax.rem(place_ref[4] + group - k, group)] = block_ref[...]
    rows, _, width = kept_ref.shape
    state = tuple(registers(came_ref[...].astype(jnp.float32)))

    def keep(row, value):
        total[row] = value + kept_ref[row]

    down_or_up(place_ref[3] != 0, place_ref[4], cost_ref, state, p1, p2, keep)
    lane = lax.broadcasted_iota(jnp.int32, (width, DISPARITIES), 1)
    index = disparity_to_lane(lane)
    for row in range(rows):
        value = total[row].T + (early_ref[:, row, :] + late_ref[:, row, :])
        out_ref[row] = jnp.take_along_axis(value, index, axis=1, mode="promise_in_bounds")


SMEM = functools.partial(pl.BlockSpec, memory_space=pltpu.SMEM)
VMEM = functools.partial(pl.BlockSpec, memory_space=pltpu.VMEM)


def call(kernel, outs, specs, scratch=(), flops=0, vmem=20):
    return pl.pallas_call(
        kernel,
        out_shape=outs,
        in_specs=specs,
        out_specs=jax.tree.map(lambda _: VMEM(), outs),
        scratch_shapes=list(scratch),
        compiler_params=pltpu.CompilerParams(vmem_limit_bytes=vmem * MEBI),
        cost_estimate=pl.CostEstimate(flops=flops, bytes_accessed=1 << 22, transcendentals=0),
    )


def spread(block, parts):
    masks, blocks = [0], [block]
    bit = parts // 2
    while bit:
        route = [(i, i ^ bit) for i in range(parts)]
        blocks += [lax.ppermute(held, "col", route) for held in blocks]
        masks += [mask ^ bit for mask in masks]
        bit //= 2
    return masks, blocks


def per_device(activations, filters, biases, present, shifts, smooth):
    _, rows, channels, width = activations.shape
    layers = filters.shape[0]
    high = rows + 2 * layers
    row_rank, row_count = lax.axis_index("row"), lax.axis_size("row")
    col_rank, parts = lax.axis_index("col"), lax.axis_size("col")
    half = row_count // 2
    cols = parts * width
    place = jnp.stack(
        [row_rank, jnp.int32(row_count), col_rank, row_rank // half, row_rank % half]
    ).astype(jnp.int32)

    downward = [(i, i + 1) for i in range(row_count - 1)]
    upward = [(i + 1, i) for i in range(row_count - 1)]
    before = lax.ppermute(activations[:, rows - layers :], "row", downward)
    after = lax.ppermute(activations[:, :layers], "row", upward)
    extra = jnp.concatenate(
        [
            present.astype(jnp.bfloat16),
            jnp.zeros((16 - rows, width), jnp.bfloat16),
            jnp.broadcast_to(shifts.astype(jnp.bfloat16), (channels - 16, width)),
        ],
        axis=0,
    )
    edges = jnp.concatenate(
        [before.reshape(-1, channels, width), after.reshape(-1, channels, width), extra[None]],
        axis=0,
    )
    masks, tiles = spread(activations.reshape(2 * rows, channels, width), parts)
    _, edges = spread(edges, parts)
    taps = jnp.transpose(filters, (0, 2, 3, 1, 4)).reshape(layers, 3 * channels, 3 * channels)

    f32, bf16 = jnp.float32, jnp.bfloat16
    lead = (OFF_MOST + 2 * width - 1) // width * width
    cost, own = call(
        functools.partial(band_kernel, masks),
        (
            jax.ShapeDtypeStruct((cols, rows, DISPARITIES), f32),
            jax.ShapeDtypeStruct((rows, DISPARITIES, width), bf16),
        ),
        [SMEM()] + [VMEM()] * (2 + 2 * parts),
        [
            pltpu.VMEM((high * channels, cols), bf16),
            pltpu.VMEM(((high - 2) * channels, cols), bf16),
            pltpu.VMEM((rows * channels, cols), bf16),
            pltpu.VMEM((rows * channels, lead + cols + width), bf16),
            pltpu.VMEM((16, cols), f32),
            pltpu.VMEM((parts, SUB, width), f32),
        ],
        flops=10**10,
        vmem=40,
    )(place, taps, biases[:, :, None], *tiles, *edges)

    blocks = [own]
    for k in range(1, half):
        turn = [(i, i // half * half + (i + k) % half) for i in range(row_count)]
        blocks.append(lax.ppermute(own, "row", turn))

    halves = (
        jax.ShapeDtypeStruct((width, rows, DISPARITIES), f32),
        jax.ShapeDtypeStruct((DISPARITIES, 2 * rows), f32),
    )
    early, state = call(
        functools.partial(across_kernel, False),
        halves,
        [SMEM(), SMEM(), VMEM()],
        flops=10**10,
    )(place, smooth, cost)
    *blocks, state = lax.optimization_barrier((*blocks, state))

    joined = pltpu.VMEM((half, rows, DISPARITIES, width), bf16)
    kept, last = call(
        first_vertical_kernel,
        (
            jax.ShapeDtypeStruct((rows, DISPARITIES, width), f32),
            jax.ShapeDtypeStruct((DISPARITIES, width), bf16),
        ),
        [SMEM(), SMEM()] + [VMEM()] * half,
        [joined],
        flops=2 * 10**9,
    )(place, smooth, *blocks)

    swap = [(i, (i + half) % row_count) for i in range(row_count)]
    last, state = lax.optimization_barrier((last, state))
    came = lax.ppermute(last, "row", swap)
    late, _ = call(
        functools.partial(across_kernel, True),
        halves,
        [SMEM(), SMEM(), VMEM(), VMEM()],
        flops=10**10,
    )(place, smooth, cost, state)

    return call(
        second_vertical_kernel,
        jax.ShapeDtypeStruct((rows, width, DISPARITIES), f32),
        [SMEM(), SMEM()] + [VMEM()] * (half + 4),
        [pltpu.VMEM((rows, DISPARITIES, width), f32), joined],
        flops=3 * 10**9,
    )(place, smooth, *blocks, kept, came, early, late)


def solution(mesh):
    return jax.shard_map(
        per_device,
        mesh=mesh,
        in_specs=(P(None, "row", None, "col"), P(), P(), P("row", "col"), P("row", "col"), P()),
        out_specs=P("row", "col", None),
        check_vma=False,
    )
```

profile of v0, /device:TPU:0, one launch (start us, length us, event | category | flops | bytes accessed | tf_op | source)
XLA Modules:
  0.0 68.7 jit_solution(3889621377067103239)
XLA Ops:
  0.0 3.0 %collective-permute-start = (bf16[16,64,128]{2,1,0:T(8,128)(2,1)}, bf16[16,64,128]{2,1,0:T(8,128)(2,1)S(1)}, u32[]{:S(2)}, u32[]{:S(2)}) collective-permute-start(bf16[16,64,128]{2,1,0:T(8,128)(2,1)} %bitcast.12), channel_id=1, source_target_pairs={{0,2},{1,3},{2,0},{3,1},{4,6},{5,7},{6,4},{7,5},{8,10},{9,11},{10,... | collective-permute-start | bytes 786440 | tf_op jit(solution)/shard_map/ppermute | solution.py:280
  3.0 1.0 %fusion = (bf16[2,3,64,128]{3,2,1,0:T(8,128)(2,1)S(1)}, bf16[2,3,64,128]{3,2,1,0:T(8,128)(2,1)S(1)}) fusion(bf16[2,8,64,128]{3,2,1,0:T(8,128)(2,1)} %param.6), kind=kLoop, calls=%fused_computation.2 | loop fusion | bytes 393216 | tf_op jit(solution)/shard_map/slice | solution.py:300
  4.0 1.3 %collective-permute-start.4 = (bf16[2,3,64,128]{3,2,1,0:T(8,128)(2,1)S(1)}, bf16[2,3,64,128]{3,2,1,0:T(8,128)(2,1)S(1)}, u32[]{:S(2)}, u32[]{:S(2)}) collective-permute-start(bf16[2,3,64,128]{3,2,1,0:T(8,128)(2,1)S(1)} %get-tuple-element.34), channel_id=1, source_target_pairs={{4,0},{8,4},{12,8},{16,12},{20,16},{24,20},{28,24},{5,1},{9,5},{13... | collective-permute-start | bytes 294920 | tf_op jit(solution)/shard_map/ppermute | solution.py:301
  5.3 4.6 %collective-permute-start.3 = (bf16[2,3,64,128]{3,2,1,0:T(8,128)(2,1)S(1)}, bf16[2,3,64,128]{3,2,1,0:T(8,128)(2,1)S(1)}, u32[]{:S(2)}, u32[]{:S(2)}) collective-permute-start(bf16[2,3,64,128]{3,2,1,0:T(8,128)(2,1)S(1)} %get-tuple-element.33), channel_id=1, source_target_pairs={{0,4},{4,8},{8,12},{12,16},{16,20},{20,24},{24,28},{1,5},{5,9},{9,... | collective-permute-start | bytes 294920 | tf_op jit(solution)/shard_map/ppermute | solution.py:300
  9.8 0.7 %convert_element_type.6 = bf16[8,128]{1,0:T(8,128)(2,1)S(1)} convert(s32[8,128]{1,0:T(8,128)} %param.9) | non-fusion elementwise | flops 1024 | bytes 6144 | tf_op jit(solution)/shard_map/convert_element_type | solution.py:304
  11.2 0.1 pad.5.clone
  11.3 0.1 pad.4.clone
  11.3 0.1 maximum_bitcast_fusion
  11.4 0.0 collective-permute-done.4
  11.4 0.9 %collective-permute-done.3 = bf16[2,3,64,128]{3,2,1,0:T(8,128)(2,1)S(1)} collective-permute-done((bf16[2,3,64,128]{3,2,1,0:T(8,128)(2,1)S(1)}, bf16[2,3,64,128]{3,2,1,0:T(8,128)(2,1)S(1)}, u32[]{:S(2)}, u32[]{:S(2)}) %collective-permute-start.3) | collective-permute-done | bytes 98336 | tf_op jit(solution)/shard_map/ppermute | solution.py:300
  12.4 0.4 collective-permute-start.5
  12.8 0.5 collective-permute-start.2
  13.3 0.0 collective-permute-start.6
  13.3 5.7 %collective-permute-done.5.refs_5_ = bf16[13,64,128]{2,1,0:T(8,128)(2,1)S(1)} collective-permute-done((bf16[13,64,128]{2,1,0:T(8,128)(2,1)S(1)}, bf16[13,64,128]{2,1,0:T(8,128)(2,1)S(1)}, u32[]{:S(2)}, u32[]{:S(2)}) %collective-permute-start.5) | collective-permute-done | bytes 213024 | tf_op jit(solution)/shard_map/ppermute | solution.py:280
  19.0 1.4 %copy.8 = bf16[3,3,64,3,64]{4,3,2,1,0:T(4,128)(2,1)S(1)} copy(bf16[3,3,64,3,64]{4,2,1,3,0:T(8,128)(2,1)} %bitcast.15) | data formatting | bytes 442368 | tf_op jit(solution)/shard_map/transpose | solution.py:316
  20.4 0.4 reshape.12.filter_ref
  20.8 0.1 copy.9.bias_ref
  20.9 0.1 stack.19.place_ref
  21.0 0.0 collective-permute-done.1.refs_2_
  21.0 0.0 collective-permute-done.6.refs_6_
  21.0 0.0 collective-permute-done.2.refs_3_
  21.0 12.1 %shard_map.64 = (f32[512,8,128]{2,1,0:T(8,128)S(1)}, bf16[8,128,128]{2,1,0:T(8,128)(2,1)S(1)}) custom-call(s32[5]{0:T(128)S(1)} %stack.19.place_ref, bf16[3,192,192]{2,1,0:T(8,128)(2,1)S(1)} %reshape.12.filter_ref, f32[3,64,1]{2,1,0:T(8,128)S(1)} %copy.9.bias_ref, bf16[16,64,128]{2,1,0:T(8,128)(2,1)S(1)} %bitcast.14, ...), custom_call_target="tpu_custom_call" | custom-call | flops 10000000000 | bytes 4194304 | tf_op jit(solution)/shard_map/pallas_call | solution.py:320
  33.2 2.5 %collective-permute-start.8 = (bf16[8,128,128]{2,1,0:T(8,128)(2,1)S(1)}, bf16[8,128,128]{2,1,0:T(8,128)(2,1)S(1)}, u32[]{:S(2)}, u32[]{:S(2)}) collective-permute-start(bf16[8,128,128]{2,1,0:T(8,128)(2,1)S(1)} %get-tuple-element.22.refs_0_), channel_id=1, source_target_pairs={{0,4},{4,8},{8,12},{12,0},{16,20},{20,24},{24,28},{28,16},{1,5},{5... | collective-permute-start | bytes 786440 | tf_op jit(solution)/shard_map/ppermute | solution.py:342
  35.7 1.6 %collective-permute-start.9 = (bf16[8,128,128]{2,1,0:T(8,128)(2,1)S(1)}, bf16[8,128,128]{2,1,0:T(8,128)(2,1)S(1)}, u32[]{:S(2)}, u32[]{:S(2)}) collective-permute-start(bf16[8,128,128]{2,1,0:T(8,128)(2,1)S(1)} %get-tuple-element.22.refs_0_), channel_id=1, source_target_pairs={{0,8},{4,12},{8,0},{12,4},{16,24},{20,28},{24,16},{28,20},{1,9},{5... | collective-permute-start | bytes 786440 | tf_op jit(solution)/shard_map/ppermute | solution.py:342
  37.3 2.0 %collective-permute-start.10 = (bf16[8,128,128]{2,1,0:T(8,128)(2,1)S(1)}, bf16[8,128,128]{2,1,0:T(8,128)(2,1)S(1)}, u32[]{:S(2)}, u32[]{:S(2)}) collective-permute-start(bf16[8,128,128]{2,1,0:T(8,128)(2,1)S(1)} %get-tuple-element.22.refs_0_), channel_id=1, source_target_pairs={{0,12},{4,0},{8,4},{12,8},{16,28},{20,16},{24,20},{28,24},{1,13},{... | collective-permute-start | bytes 786440 | tf_op jit(solution)/shard_map/ppermute | solution.py:342
  39.3 11.0 %shard_map.65 = (f32[128,8,128]{2,1,0:T(8,128)S(1)}, f32[128,16]{1,0:T(8,128)S(1)}) custom-call(s32[5]{0:T(128)S(1)} %stack.19.place_ref, s32[2]{0:T(128)S(1)} %copy-done.1, f32[512,8,128]{2,1,0:T(8,128)S(1)} %get-tuple-element.20.cost_ref), custom_call_target="tpu_custom_call" | custom-call | flops 10000000000 | bytes 4194304 | tf_op jit(solution)/shard_map/pallas_call | solution.py:348
  50.3 0.0 collective-permute-done.8.refs_1_
  50.3 0.0 collective-permute-done.10.refs_3_
  50.3 1.3 %shard_map.66 = (f32[8,128,128]{2,1,0:T(8,128)S(1)}, bf16[128,128]{1,0:T(8,128)(2,1)S(1)}) custom-call(s32[5]{0:T(128)S(1)} %stack.19.place_ref, s32[2]{0:T(128)S(1)} %copy-done.1, bf16[8,128,128]{2,1,0:T(8,128)(2,1)S(1)} %get-tuple-element.22.refs_0_, bf16[8,128,128]{2,1,0:T(8,128)(2,1)S(1)} %collective-permute-done.8.refs_1_, ...), custom_call_target="tpu_custom_call" | custom-call | flops 2000000000 | bytes 4194304 | tf_op jit(solution)/shard_map/pallas_call | solution.py:357
  51.6 2.7 %collective-permute-start.11 = (bf16[128,128]{1,0:T(8,128)(2,1)S(1)}, bf16[128,128]{1,0:T(8,128)(2,1)S(1)}, u32[]{:S(2)}, u32[]{:S(2)}) collective-permute-start(bf16[128,128]{1,0:T(8,128)(2,1)S(1)} %get-tuple-element.29), channel_id=1, source_target_pairs={{0,16},{4,20},{8,24},{12,28},{16,0},{20,4},{24,8},{28,12},{1,17},{... | collective-permute-start | bytes 98312 | tf_op jit(solution)/shard_map/ppermute | solution.py:370
  54.3 11.6 %shard_map.67 = (f32[128,8,128]{2,1,0:T(8,128)S(1)}, f32[128,16]{1,0:T(8,128)}) custom-call(s32[5]{0:T(128)S(1)} %stack.19.place_ref, s32[2]{0:T(128)S(1)} %copy-done.1, f32[512,8,128]{2,1,0:T(8,128)S(1)} %get-tuple-element.20.cost_ref, f32[128,16]{1,0:T(8,128)S(1)} %get-tuple-element.31.refs_0_), custom_call_target="tpu_custom_call" | custom-call | flops 10000000000 | bytes 4194304 | tf_op jit(solution)/shard_map/pallas_call | solution.py:371
  65.9 2.7 %shard_map.68 = f32[8,128,128]{2,1,0:T(8,128)} custom-call(s32[5]{0:T(128)S(1)} %stack.19.place_ref, s32[2]{0:T(128)S(1)} %copy-done.1, bf16[8,128,128]{2,1,0:T(8,128)(2,1)S(1)} %get-tuple-element.22.refs_0_, bf16[8,128,128]{2,1,0:T(8,128)(2,1)S(1)} %collective-permute-done.8.refs_1_, bf16[8,128,128]{2,1,0:T(8,128)(2,1)S(1)} %collective-permute-done.9.refs_2_, ...), custom_call_target="tpu_custom_call" | custom-call | flops 3000000000 | bytes 4194304 | tf_op jit(solution)/shard_map/pallas_call | solution.py:378
  (15 shorter events, 0.1 us)
Async XLA Ops:
  0.0 21.0 %copy-start = (bf16[2,8,64,128]{3,2,1,0:T(8,128)(2,1)S(1)}, bf16[2,8,64,128]{3,2,1,0:T(8,128)(2,1)}, u32[]{:S(2)}) copy-start(bf16[2,8,64,128]{3,2,1,0:T(8,128)(2,1)} %param.6) | copy-start | bytes 786436
  0.0 20.8 %copy-start.2 = (f32[3,64]{1,0:T(4,128)S(1)}, f32[3,64]{1,0:T(4,128)}, u32[]{:S(2)}) copy-start(f32[3,64]{1,0:T(4,128)} %param.8) | copy-start | bytes 2308
  0.0 12.8 %collective-permute-start = (bf16[16,64,128]{2,1,0:T(8,128)(2,1)}, bf16[16,64,128]{2,1,0:T(8,128)(2,1)S(1)}, u32[]{:S(2)}, u32[]{:S(2)}) collective-permute-start(bf16[16,64,128]{2,1,0:T(8,128)(2,1)} %bitcast.12), channel_id=1, source_target_pairs={{0,2},{1,3},{2,0},{3,1},{4,6},{5,7},{6,4},{7,5},{8,10},{9,11},{10,... | collective-permute-start | bytes 786440 | tf_op jit(solution)/shard_map/ppermute | solution.py:280
  4.0 7.5 %collective-permute-start.4 = (bf16[2,3,64,128]{3,2,1,0:T(8,128)(2,1)S(1)}, bf16[2,3,64,128]{3,2,1,0:T(8,128)(2,1)S(1)}, u32[]{:S(2)}, u32[]{:S(2)}) collective-permute-start(bf16[2,3,64,128]{3,2,1,0:T(8,128)(2,1)S(1)} %get-tuple-element.34), channel_id=1, source_target_pairs={{4,0},{8,4},{12,8},{16,12},{20,16},{24,20},{28,24},{5,1},{9,5},{13... | collective-permute-start | bytes 294920 | tf_op jit(solution)/shard_map/ppermute | solution.py:301
  5.3 7.1 %collective-permute-start.3 = (bf16[2,3,64,128]{3,2,1,0:T(8,128)(2,1)S(1)}, bf16[2,3,64,128]{3,2,1,0:T(8,128)(2,1)S(1)}, u32[]{:S(2)}, u32[]{:S(2)}) collective-permute-start(bf16[2,3,64,128]{3,2,1,0:T(8,128)(2,1)S(1)} %get-tuple-element.33), channel_id=1, source_target_pairs={{0,4},{4,8},{8,12},{12,16},{16,20},{20,24},{24,28},{1,5},{5,9},{9,... | collective-permute-start | bytes 294920 | tf_op jit(solution)/shard_map/ppermute | solution.py:300
  12.4 6.6 %collective-permute-start.5 = (bf16[13,64,128]{2,1,0:T(8,128)(2,1)S(1)}, bf16[13,64,128]{2,1,0:T(8,128)(2,1)S(1)}, u32[]{:S(2)}, u32[]{:S(2)}) collective-permute-start(bf16[13,64,128]{2,1,0:T(8,128)(2,1)S(1)} %pad_maximum_fusion.refs_4_), channel_id=1, source_target_pairs={{0,2},{1,3},{2,0},{3,1},{4,6},{5,7},{6,4},{7,5},{8,10},{9,11},{10,... | collective-permute-start | bytes 638984 | tf_op jit(solution)/shard_map/ppermute | solution.py:280
  12.8 8.2 %collective-permute-start.1 = (bf16[16,64,128]{2,1,0:T(8,128)(2,1)}, bf16[16,64,128]{2,1,0:T(8,128)(2,1)S(1)}, u32[]{:S(2)}, u32[]{:S(2)}) collective-permute-start(bf16[16,64,128]{2,1,0:T(8,128)(2,1)} %bitcast.13), channel_id=1, source_target_pairs={{0,1},{1,0},{2,3},{3,2},{4,5},{5,4},{6,7},{7,6},{8,9},{9,8},{10,11... | collective-permute-start | bytes 786440 | tf_op jit(solution)/shard_map/ppermute | solution.py:280
  12.8 8.2 %collective-permute-start.2 = (bf16[16,64,128]{2,1,0:T(8,128)(2,1)S(1)}, bf16[16,64,128]{2,1,0:T(8,128)(2,1)S(1)}, u32[]{:S(2)}, u32[]{:S(2)}) collective-permute-start(bf16[16,64,128]{2,1,0:T(8,128)(2,1)S(1)} %collective-permute-done.refs_1_), channel_id=1, source_target_pairs={{0,1},{1,0},{2,3},{3,2},{4,5},{5,4},{6,7},{7,6},{8,9},{9,8},{10,11... | collective-permute-start | bytes 786440 | tf_op jit(solution)/shard_map/ppermute | solution.py:280
  13.3 7.7 %collective-permute-start.6 = (bf16[13,64,128]{2,1,0:T(8,128)(2,1)S(1)}, bf16[13,64,128]{2,1,0:T(8,128)(2,1)S(1)}, u32[]{:S(2)}, u32[]{:S(2)}) collective-permute-start(bf16[13,64,128]{2,1,0:T(8,128)(2,1)S(1)} %pad_maximum_fusion.refs_4_), channel_id=1, source_target_pairs={{0,1},{1,0},{2,3},{3,2},{4,5},{5,4},{6,7},{7,6},{8,9},{9,8},{10,11... | collective-permute-start | bytes 638984 | tf_op jit(solution)/shard_map/ppermute | solution.py:280
  19.0 2.0 %collective-permute-start.7 = (bf16[13,64,128]{2,1,0:T(8,128)(2,1)S(1)}, bf16[13,64,128]{2,1,0:T(8,128)(2,1)S(1)}, u32[]{:S(2)}, u32[]{:S(2)}) collective-permute-start(bf16[13,64,128]{2,1,0:T(8,128)(2,1)S(1)} %collective-permute-done.5.refs_5_), channel_id=1, source_target_pairs={{0,1},{1,0},{2,3},{3,2},{4,5},{5,4},{6,7},{7,6},{8,9},{9,8},{10,11... | collective-permute-start | bytes 638984 | tf_op jit(solution)/shard_map/ppermute | solution.py:280
  21.0 18.3 %copy-start.1 = (s32[2]{0:T(128)S(1)}, s32[2]{0:T(128)}, u32[]{:S(2)}) copy-start(s32[2]{0:T(128)} %charge_ref.7) | copy-start | bytes 28
  33.2 17.1 %collective-permute-start.8 = (bf16[8,128,128]{2,1,0:T(8,128)(2,1)S(1)}, bf16[8,128,128]{2,1,0:T(8,128)(2,1)S(1)}, u32[]{:S(2)}, u32[]{:S(2)}) collective-permute-start(bf16[8,128,128]{2,1,0:T(8,128)(2,1)S(1)} %get-tuple-element.22.refs_0_), channel_id=1, source_target_pairs={{0,4},{4,8},{8,12},{12,0},{16,20},{20,24},{24,28},{28,16},{1,5},{5... | collective-permute-start | bytes 786440 | tf_op jit(solution)/shard_map/ppermute | solution.py:342
  35.7 14.6 %collective-permute-start.9 = (bf16[8,128,128]{2,1,0:T(8,128)(2,1)S(1)}, bf16[8,128,128]{2,1,0:T(8,128)(2,1)S(1)}, u32[]{:S(2)}, u32[]{:S(2)}) collective-permute-start(bf16[8,128,128]{2,1,0:T(8,128)(2,1)S(1)} %get-tuple-element.22.refs_0_), channel_id=1, source_target_pairs={{0,8},{4,12},{8,0},{12,4},{16,24},{20,28},{24,16},{28,20},{1,9},{5... | collective-permute-start | bytes 786440 | tf_op jit(solution)/shard_map/ppermute | solution.py:342
  37.3 13.0 %collective-permute-start.10 = (bf16[8,128,128]{2,1,0:T(8,128)(2,1)S(1)}, bf16[8,128,128]{2,1,0:T(8,128)(2,1)S(1)}, u32[]{:S(2)}, u32[]{:S(2)}) collective-permute-start(bf16[8,128,128]{2,1,0:T(8,128)(2,1)S(1)} %get-tuple-element.22.refs_0_), channel_id=1, source_target_pairs={{0,12},{4,0},{8,4},{12,8},{16,28},{20,16},{24,20},{28,24},{1,13},{... | collective-permute-start | bytes 786440 | tf_op jit(solution)/shard_map/ppermute | solution.py:342
  51.6 14.3 %collective-permute-start.11 = (bf16[128,128]{1,0:T(8,128)(2,1)S(1)}, bf16[128,128]{1,0:T(8,128)(2,1)S(1)}, u32[]{:S(2)}, u32[]{:S(2)}) collective-permute-start(bf16[128,128]{1,0:T(8,128)(2,1)S(1)} %get-tuple-element.29), channel_id=1, source_target_pairs={{0,16},{4,20},{8,24},{12,28},{16,0},{20,4},{24,8},{28,12},{1,17},{... | collective-permute-start | bytes 98312 | tf_op jit(solution)/shard_map/ppermute | solution.py:370
where the time goes:
time: 68.9 us; the launch traced here: 68.7 us
  Pallas kernels  38.8 us (56%)
  starting transfers between devices  18.5 us (27%)
  waiting for transfers between devices  6.62 us (10%)
  local copies, waits for them, and re-layouts  3.1 us (4%)
  other arithmetic  0.81 us (1%)
  between operations  0.81 us (1%)
    pallas_call x1, Pallas kernels, per_device(): call(functools.partial(band_kernel, masks), (jax.ShapeDtypeStruct((cols,...  12.1 us
    pallas_call x1, Pallas kernels, per_device(): call(functools.partial(across_kernel, True), halves, [SMEM(), SMEM(), VME...  11.6 us
    pallas_call x1, Pallas kernels, per_device(): call(functools.partial(across_kernel, False), halves, [SMEM(), SMEM(), VM...  11 us
    ppermute x3, starting transfers between devices, per_device(): blocks.append(lax.ppermute(own, 'row', turn))  6.13 us
    ppermute x6, waiting for transfers between devices, spread(): blocks += [lax.ppermute(held, 'col', route) for held in blocks]  5.7 us
    ppermute x1, starting transfers between devices, per_device(): before = lax.ppermute(activations[:, rows - layers:], 'row', downward)  4.55 us
    ppermute x6, starting transfers between devices, spread(): blocks += [lax.ppermute(held, 'col', route) for held in blocks]  3.9 us
    pallas_call x1, Pallas kernels, per_device(): call(second_vertical_kernel, jax.ShapeDtypeStruct((rows, width, DISPARITI...  2.75 us
  transfers between devices with their start and end apart: 12, of which 2 were waited for; matrix products, arithmetic and copies ran while one was open for 6% of the time, Pallas kernels for 33%

commit v1 on v0

--- a/solution.py
+++ b/solution.py
@@ -22,26 +22,36 @@
     return (disparity % REGS) * SUB + disparity // REGS
 
 
-def advance(state, cost, p1, p2):
-    lanes = state[0].shape[1]
-    row = lax.broadcasted_iota(jnp.int32, (SUB, lanes), 0)
+def least_of(values):
+    while len(values) > 1:
+        values = [jnp.minimum(a, b) for a, b in zip(values[::2], values[1::2])]
+    turned = values + [pltpu.roll(values[0], turn, 0) for turn in range(1, SUB)]
+    while len(turned) > 1:
+        turned = [jnp.minimum(a, b) for a, b in zip(turned[::2], turned[1::2])]
+    return turned[0]
+
+
+def stepped(state, p1):
+    row = lax.broadcasted_iota(jnp.int32, state[0].shape, 0)
     below = jnp.where(row == 0, jnp.inf, pltpu.roll(state[-1], 1, 0))
     above = jnp.where(row == SUB - 1, jnp.inf, pltpu.roll(state[0], SUB - 1, 0))
-    least = list(state)
-    while len(least) > 1:
-        least = [jnp.minimum(a, b) for a, b in zip(least[::2], least[1::2])]
-    least = least[0]
-    turned = [least] + [pltpu.roll(least, turn, 0) for turn in range(1, SUB)]
-    while len(turned) > 1:
-        turned = [jnp.minimum(a, b) for a, b in zip(turned[::2], turned[1::2])]
-    least = turned[0]
     lower = [below] + state[:-1]
     upper = state[1:] + [above]
-    fresh = []
-    for s, l, u, c in zip(state, lower, upper, cost):
-        t = jnp.minimum(s, jnp.minimum(l, u) + p1)
-        fresh.append(c + jnp.minimum(t - least, p2))
-    return fresh
+    return [
+        jnp.minimum(s, jnp.minimum(l, u) + p1) for s, l, u in zip(state, lower, upper)
+    ]
+
+
+def advance(state, cost, p1, p2):
+    least = least_of(state)
+    return [c + jnp.minimum(t - least, p2) for t, c in zip(stepped(state, p1), cost)]
+
+
+def advance_ahead(sums, jump, cost, p1, p2):
+    walked = [c + t for t, c in zip(stepped(sums, p1), cost)]
+    fresh = [jnp.minimum(w, c + jump) for w, c in zip(walked, cost)]
+    following = jnp.minimum(least_of(walked) + p2, (least_of(cost) + p2) + jump)
+    return fresh, following
 
 
 def charges(charge_ref):
@@ -58,7 +68,7 @@
 def band_kernel(masks, place_ref, filter_ref, bias_ref, *refs):
     parts = len(masks)
     tile_refs, edge_refs, refs = refs[:parts], refs[parts : 2 * parts], refs[2 * parts :]
-    cost_ref, own_ref, maps_a, maps_b, left_unit, right_unit, present, shifts = refs
+    cost_ref, own_ref, maps_a, maps_b, left_unit, right_unit, present, shifts, taps_ref = refs
     _, channels, width = tile_refs[0].shape
     layers = filter_ref.shape[0]
     rows = own_ref.shape[0]
@@ -68,6 +78,13 @@
     rows_total = place_ref[1] * rows
     own = place_ref[2]
     lead = (OFF_MOST + 2 * width - 1) // width * width
+
+    for layer in range(layers):
+        for a in range(3):
+            for b in range(3):
+                taps_ref[
+                    layer, b * channels : (b + 1) * channels, a * channels : (a + 1) * channels
+                ] = filter_ref[layer, a, b]
 
     for mask, edge_ref in zip(masks, edge_refs):
         member = own ^ mask
@@ -101,7 +118,7 @@
             def _(row):
                 start = pl.multiple_of(row * channels, channels)
                 window = source[pl.ds(start, 3 * channels), :]
-                taps = jnp.dot(filter_ref[layer], window, preferred_element_type=jnp.float32)
+                taps = jnp.dot(taps_ref[layer], window, preferred_element_type=jnp.float32)
                 before = pltpu.roll(taps[:channels], 1, 1)
                 after = pltpu.roll(taps[2 * channels :], cols - 1, 1)
                 z = taps[channels : 2 * channels] + jnp.where(column == 0, 0.0, before)
@@ -161,24 +178,32 @@
     own = place_ref[2]
     p1, p2 = charges(charge_ref)
 
+    def cost_at(step):
+        step = jnp.minimum(step, cols - 1)
+        pair = [cost_ref[step], cost_ref[cols - 1 - step]]
+        return registers(jnp.concatenate(pair, axis=0).T)
+
     def segment(p, state):
-        first_col = p * width
-        last_col = cols - 1 - p * width
+        first_step = p * width
 
         def run(keep_right, keep_left, state):
-            def body(i, state):
-                pair = [cost_ref[first_col + i], cost_ref[last_col - i]]
-                cost = jnp.concatenate(pair, axis=0).T
-                fresh = advance(list(state), registers(cost), p1, p2)
+            def body(i, carry):
+                sums, jump, cost = carry
+                ahead = cost_at(first_step + i + 1)
+                fresh, following = advance_ahead(list(sums), jump, list(cost), p1, p2)
                 if keep_right or keep_left:
-                    back = jnp.concatenate(fresh, axis=0).T
+                    base = jump - p2
+                    back = jnp.concatenate([f - base for f in fresh], axis=0).T
                 if keep_right:
                     kept_ref[i] = back[0:rows]
                 if keep_left:
                     kept_ref[width - 1 - i] = back[rows : 2 * rows]
-                return tuple(fresh)
-
-            return lax.fori_loop(0, width, body, state, unroll=16)
+                return tuple(fresh), following, tuple(ahead)
+
+            level = jnp.zeros((SUB, 2 * rows), jnp.float32) + p2
+            carry = (state, level, tuple(cost_at(first_step)))
+            sums, jump, _ = lax.fori_loop(0, width, body, carry, unroll=16)
+            return tuple(s - (jump - p2) for s in sums)
 
         choice = jnp.where(p == own, 1, 0) + jnp.where(parts - 1 - p == own, 2, 0)
         return lax.switch(
@@ -313,7 +338,6 @@
     )
     masks, tiles = spread(activations.reshape(2 * rows, channels, width), parts)
     _, edges = spread(edges, parts)
-    taps = jnp.transpose(filters, (0, 2, 3, 1, 4)).reshape(layers, 3 * channels, 3 * channels)
 
     f32, bf16 = jnp.float32, jnp.bfloat16
     lead = (OFF_MOST + 2 * width - 1) // width * width
@@ -331,10 +355,11 @@
             pltpu.VMEM((rows * channels, lead + cols + width), bf16),
             pltpu.VMEM((16, cols), f32),
             pltpu.VMEM((parts, SUB, width), f32),
+            pltpu.VMEM((layers, 3 * channels, 3 * channels), bf16),
         ],
         flops=10**10,
         vmem=40,
-    )(place, taps, biases[:, :, None], *tiles, *edges)
+    )(place, filters, biases[:, :, None], *tiles, *edges)
 
     blocks = [own]
     for k in range(1, half):

time: 68.9 us -> 68.5 us (level)
  Pallas kernels: 38.8 us -> 36.2 us
  local copies, waits for them, and re-layouts: 3.1 us -> 3.98 us
  starting transfers between devices: 18.5 us -> 19.2 us
    unnamed x6, local copies, waits for them, and re-layouts: 0.01 us -> 1.97 us
    transpose x1 -> x0, local copies, waits for them, and re-layouts: 1.4 us -> none  [per_device(): jnp.transpose(filters, (0, 2, 3, 1, 4))]
    pallas_call x1, Pallas kernels: 11 us -> 9.63 us  [per_device(): call(functools.partial(across_kernel, False), halves, [SMEM(), SMEM(), VM...]
    pallas_call x1, Pallas kernels: 11.6 us -> 10.3 us  [per_device(): call(functools.partial(across_kernel, True), halves, [SMEM(), SMEM(), VME...]
    ppermute x1, starting transfers between devices: 2.66 us -> 3.35 us  [per_device(): came = lax.ppermute(last, 'row', swap)]
  transfers between devices with their start and end apart: 12 -> 12, of which waited for: 2 -> 3; matrix products, arithmetic and copies ran while one was open for 6% -> 4% of each run, Pallas kernels for 33% -> 29%
where the time goes in v1:
time: 68.5 us; the launch traced here: 68.2 us
  Pallas kernels  36.2 us (53%)
  starting transfers between devices  19.2 us (28%)
  waiting for transfers between devices  7.23 us (11%)
  local copies, waits for them, and re-layouts  3.98 us (6%)
  other arithmetic  0.81 us (1%)
  between operations  0.79 us (1%)
    pallas_call x1, Pallas kernels, per_device(): call(functools.partial(band_kernel, masks), (jax.ShapeDtypeStruct((cols,...  12.2 us
    pallas_call x1, Pallas kernels, per_device(): call(functools.partial(across_kernel, True), halves, [SMEM(), SMEM(), VME...  10.3 us
    pallas_call x1, Pallas kernels, per_device(): call(functools.partial(across_kernel, False), halves, [SMEM(), SMEM(), VM...  9.63 us
    ppermute x6, waiting for transfers between devices, spread(): blocks += [lax.ppermute(held, 'col', route) for held in blocks]  6.31 us
    ppermute x3, starting transfers between devices, per_device(): blocks.append(lax.ppermute(own, 'row', turn))  6.16 us
    ppermute x1, starting transfers between devices, per_device(): before = lax.ppermute(activations[:, rows - layers:], 'row', downward)  4.55 us
    ppermute x6, starting transfers between devices, spread(): blocks += [lax.ppermute(held, 'col', route) for held in blocks]  3.84 us
    ppermute x1, starting transfers between devices, per_device(): came = lax.ppermute(last, 'row', swap)  3.35 us
  transfers between devices with their start and end apart: 12, of which 3 were waited for; matrix products, arithmetic and copies ran while one was open for 4% of the time, Pallas kernels for 29%

profile of v1, /device:TPU:0, one launch (start us, length us, event | category | flops | bytes accessed | tf_op | source)
XLA Modules:
  0.0 68.2 jit_solution(8766324260111569342)
XLA Ops:
  0.0 3.0 %collective-permute-start = (bf16[16,64,128]{2,1,0:T(8,128)(2,1)}, bf16[16,64,128]{2,1,0:T(8,128)(2,1)S(1)}, u32[]{:S(2)}, u32[]{:S(2)}) collective-permute-start(bf16[16,64,128]{2,1,0:T(8,128)(2,1)} %bitcast.11), channel_id=1, source_target_pairs={{0,2},{1,3},{2,0},{3,1},{4,6},{5,7},{6,4},{7,5},{8,10},{9,11},{10,... | collective-permute-start | bytes 786440 | tf_op jit(solution)/shard_map/ppermute | solution.py:305
  3.0 1.0 %fusion = (bf16[2,3,64,128]{3,2,1,0:T(8,128)(2,1)S(1)}, bf16[2,3,64,128]{3,2,1,0:T(8,128)(2,1)S(1)}) fusion(bf16[2,8,64,128]{3,2,1,0:T(8,128)(2,1)} %param.6), kind=kLoop, calls=%fused_computation.2 | loop fusion | bytes 393216 | tf_op jit(solution)/shard_map/slice | solution.py:325
  3.9 1.3 %collective-permute-start.4 = (bf16[2,3,64,128]{3,2,1,0:T(8,128)(2,1)S(1)}, bf16[2,3,64,128]{3,2,1,0:T(8,128)(2,1)S(1)}, u32[]{:S(2)}, u32[]{:S(2)}) collective-permute-start(bf16[2,3,64,128]{3,2,1,0:T(8,128)(2,1)S(1)} %get-tuple-element.34), channel_id=1, source_target_pairs={{4,0},{8,4},{12,8},{16,12},{20,16},{24,20},{28,24},{5,1},{9,5},{13... | collective-permute-start | bytes 294920 | tf_op jit(solution)/shard_map/ppermute | solution.py:326
  5.2 4.6 %collective-permute-start.3 = (bf16[2,3,64,128]{3,2,1,0:T(8,128)(2,1)S(1)}, bf16[2,3,64,128]{3,2,1,0:T(8,128)(2,1)S(1)}, u32[]{:S(2)}, u32[]{:S(2)}) collective-permute-start(bf16[2,3,64,128]{3,2,1,0:T(8,128)(2,1)S(1)} %get-tuple-element.33), channel_id=1, source_target_pairs={{0,4},{4,8},{8,12},{12,16},{16,20},{20,24},{24,28},{1,5},{5,9},{9,... | collective-permute-start | bytes 294920 | tf_op jit(solution)/shard_map/ppermute | solution.py:325
  9.8 0.7 %convert_element_type.6 = bf16[8,128]{1,0:T(8,128)(2,1)S(1)} convert(s32[8,128]{1,0:T(8,128)} %param.9) | non-fusion elementwise | flops 1024 | bytes 6144 | tf_op jit(solution)/shard_map/convert_element_type | solution.py:329
  11.2 0.1 pad.5.clone
  11.2 0.1 pad.4.clone
  11.3 0.1 maximum_bitcast_fusion
  11.4 0.0 collective-permute-done.4
  11.4 0.9 %collective-permute-done.3 = bf16[2,3,64,128]{3,2,1,0:T(8,128)(2,1)S(1)} collective-permute-done((bf16[2,3,64,128]{3,2,1,0:T(8,128)(2,1)S(1)}, bf16[2,3,64,128]{3,2,1,0:T(8,128)(2,1)S(1)}, u32[]{:S(2)}, u32[]{:S(2)}) %collective-permute-start.3) | collective-permute-done | bytes 98336 | tf_op jit(solution)/shard_map/ppermute | solution.py:325
  12.4 0.4 collective-permute-start.5
  12.7 0.0 collective-permute-start.1
  12.7 0.0 collective-permute-done.refs_1_
  12.7 0.5 collective-permute-start.2
  13.2 0.0 collective-permute-start.6
  13.2 5.8 %collective-permute-done.5.refs_5_ = bf16[13,64,128]{2,1,0:T(8,128)(2,1)S(1)} collective-permute-done((bf16[13,64,128]{2,1,0:T(8,128)(2,1)S(1)}, bf16[13,64,128]{2,1,0:T(8,128)(2,1)S(1)}, u32[]{:S(2)}, u32[]{:S(2)}) %collective-permute-start.5) | collective-permute-done | bytes 213024 | tf_op jit(solution)/shard_map/ppermute | solution.py:305
  19.0 0.0 collective-permute-start.7
  19.0 0.8 %copy.7.bias_ref = f32[3,64,1]{2,1,0:T(8,128)S(1)} copy(f32[3,64,1]{1,0,2:T(4,128)} %bitcast.16) | data formatting | bytes 1536 | tf_op jit(solution)/shard_map/broadcast_in_dim | solution.py:362
  19.8 0.0 copy-start.2
  19.8 0.1 stack.19.place_ref
  19.9 0.5 collective-permute-done.7.refs_7_
  20.5 0.9 %copy-done = bf16[2,8,64,128]{3,2,1,0:T(8,128)(2,1)S(1)} copy-done((bf16[2,8,64,128]{3,2,1,0:T(8,128)(2,1)S(1)}, bf16[2,8,64,128]{3,2,1,0:T(8,128)(2,1)}, u32[]{:S(2)}) %copy-start) | copy-done | bytes 262168
  21.4 1.0 %copy-done.1 = bf16[3,3,3,64,64]{4,3,2,1,0:T(8,128)(2,1)S(1)} copy-done((bf16[3,3,3,64,64]{4,3,2,1,0:T(8,128)(2,1)S(1)}, bf16[3,3,3,64,64]{4,3,2,1,0:T(8,128)(2,1)}, u32[]{:S(2)}) %copy-start.1) | copy-done | bytes 221208
  22.4 12.2 %shard_map.64 = (f32[512,8,128]{2,1,0:T(8,128)S(1)}, bf16[8,128,128]{2,1,0:T(8,128)(2,1)S(1)}) custom-call(s32[5]{0:T(128)S(1)} %stack.19.place_ref, bf16[3,3,3,64,64]{4,3,2,1,0:T(8,128)(2,1)S(1)} %copy-done.1, f32[3,64,1]{2,1,0:T(8,128)S(1)} %copy.7.bias_ref, bf16[16,64,128]{2,1,0:T(8,128)(2,1)S(1)} %bitcast.13, ...), custom_call_target="tpu_custom_call" | custom-call | flops 10000000000 | bytes 4194304 | tf_op jit(solution)/shard_map/pallas_call | solution.py:344
  34.6 2.5 %collective-permute-start.8 = (bf16[8,128,128]{2,1,0:T(8,128)(2,1)S(1)}, bf16[8,128,128]{2,1,0:T(8,128)(2,1)S(1)}, u32[]{:S(2)}, u32[]{:S(2)}) collective-permute-start(bf16[8,128,128]{2,1,0:T(8,128)(2,1)S(1)} %get-tuple-element.22.refs_0_), channel_id=1, source_target_pairs={{0,4},{4,8},{8,12},{12,0},{16,20},{20,24},{24,28},{28,16},{1,5},{5... | collective-permute-start | bytes 786440 | tf_op jit(solution)/shard_map/ppermute | solution.py:367
  37.2 1.6 %collective-permute-start.9 = (bf16[8,128,128]{2,1,0:T(8,128)(2,1)S(1)}, bf16[8,128,128]{2,1,0:T(8,128)(2,1)S(1)}, u32[]{:S(2)}, u32[]{:S(2)}) collective-permute-start(bf16[8,128,128]{2,1,0:T(8,128)(2,1)S(1)} %get-tuple-element.22.refs_0_), channel_id=1, source_target_pairs={{0,8},{4,12},{8,0},{12,4},{16,24},{20,28},{24,16},{28,20},{1,9},{5... | collective-permute-start | bytes 786440 | tf_op jit(solution)/shard_map/ppermute | solution.py:367
  38.7 2.0 %collective-permute-start.10 = (bf16[8,128,128]{2,1,0:T(8,128)(2,1)S(1)}, bf16[8,128,128]{2,1,0:T(8,128)(2,1)S(1)}, u32[]{:S(2)}, u32[]{:S(2)}) collective-permute-start(bf16[8,128,128]{2,1,0:T(8,128)(2,1)S(1)} %get-tuple-element.22.refs_0_), channel_id=1, source_target_pairs={{0,12},{4,0},{8,4},{12,8},{16,28},{20,16},{24,20},{28,24},{1,13},{... | collective-permute-start | bytes 786440 | tf_op jit(solution)/shard_map/ppermute | solution.py:367
  40.8 9.6 %shard_map.65 = (f32[128,8,128]{2,1,0:T(8,128)S(1)}, f32[128,16]{1,0:T(8,128)S(1)}) custom-call(s32[5]{0:T(128)S(1)} %stack.19.place_ref, s32[2]{0:T(128)S(1)} %copy-done.2, f32[512,8,128]{2,1,0:T(8,128)S(1)} %get-tuple-element.20.cost_ref), custom_call_target="tpu_custom_call" | custom-call | flops 10000000000 | bytes 4194304 | tf_op jit(solution)/shard_map/pallas_call | solution.py:373
  50.4 1.3 %shard_map.66 = (f32[8,128,128]{2,1,0:T(8,128)S(1)}, bf16[128,128]{1,0:T(8,128)(2,1)S(1)}) custom-call(s32[5]{0:T(128)S(1)} %stack.19.place_ref, s32[2]{0:T(128)S(1)} %copy-done.2, bf16[8,128,128]{2,1,0:T(8,128)(2,1)S(1)} %get-tuple-element.22.refs_0_, bf16[8,128,128]{2,1,0:T(8,128)(2,1)S(1)} %collective-permute-done.8.refs_1_, ...), custom_call_target="tpu_custom_call" | custom-call | flops 2000000000 | bytes 4194304 | tf_op jit(solution)/shard_map/pallas_call | solution.py:382
  51.8 3.4 %collective-permute-start.11 = (bf16[128,128]{1,0:T(8,128)(2,1)S(1)}, bf16[128,128]{1,0:T(8,128)(2,1)S(1)}, u32[]{:S(2)}, u32[]{:S(2)}) collective-permute-start(bf16[128,128]{1,0:T(8,128)(2,1)S(1)} %get-tuple-element.29), channel_id=1, source_target_pairs={{0,16},{4,20},{8,24},{12,28},{16,0},{20,4},{24,8},{28,12},{1,17},{... | collective-permute-start | bytes 98312 | tf_op jit(solution)/shard_map/ppermute | solution.py:395
  55.1 10.3 %shard_map.67 = (f32[128,8,128]{2,1,0:T(8,128)S(1)}, f32[128,16]{1,0:T(8,128)}) custom-call(s32[5]{0:T(128)S(1)} %stack.19.place_ref, s32[2]{0:T(128)S(1)} %copy-done.2, f32[512,8,128]{2,1,0:T(8,128)S(1)} %get-tuple-element.20.cost_ref, f32[128,16]{1,0:T(8,128)S(1)} %get-tuple-element.31.refs_0_), custom_call_target="tpu_custom_call" | custom-call | flops 10000000000 | bytes 4194304 | tf_op jit(solution)/shard_map/pallas_call | solution.py:396
  65.4 2.8 %shard_map.68 = f32[8,128,128]{2,1,0:T(8,128)} custom-call(s32[5]{0:T(128)S(1)} %stack.19.place_ref, s32[2]{0:T(128)S(1)} %copy-done.2, bf16[8,128,128]{2,1,0:T(8,128)(2,1)S(1)} %get-tuple-element.22.refs_0_, bf16[8,128,128]{2,1,0:T(8,128)(2,1)S(1)} %collective-permute-done.8.refs_1_, bf16[8,128,128]{2,1,0:T(8,128)(2,1)S(1)} %collective-permute-done.9.refs_2_, ...), custom_call_target="tpu_custom_call" | custom-call | flops 3000000000 | bytes 4194304 | tf_op jit(solution)/shard_map/pallas_call | solution.py:403
  (13 shorter events, 0.1 us)
Async XLA Ops:
  0.0 12.7 %collective-permute-start = (bf16[16,64,128]{2,1,0:T(8,128)(2,1)}, bf16[16,64,128]{2,1,0:T(8,128)(2,1)S(1)}, u32[]{:S(2)}, u32[]{:S(2)}) collective-permute-start(bf16[16,64,128]{2,1,0:T(8,128)(2,1)} %bitcast.11), channel_id=1, source_target_pairs={{0,2},{1,3},{2,0},{3,1},{4,6},{5,7},{6,4},{7,5},{8,10},{9,11},{10,... | collective-permute-start | bytes 786440 | tf_op jit(solution)/shard_map/ppermute | solution.py:305
  3.9 7.5 %collective-permute-start.4 = (bf16[2,3,64,128]{3,2,1,0:T(8,128)(2,1)S(1)}, bf16[2,3,64,128]{3,2,1,0:T(8,128)(2,1)S(1)}, u32[]{:S(2)}, u32[]{:S(2)}) collective-permute-start(bf16[2,3,64,128]{3,2,1,0:T(8,128)(2,1)S(1)} %get-tuple-element.34), channel_id=1, source_target_pairs={{4,0},{8,4},{12,8},{16,12},{20,16},{24,20},{28,24},{5,1},{9,5},{13... | collective-permute-start | bytes 294920 | tf_op jit(solution)/shard_map/ppermute | solution.py:326
  5.2 7.1 %collective-permute-start.3 = (bf16[2,3,64,128]{3,2,1,0:T(8,128)(2,1)S(1)}, bf16[2,3,64,128]{3,2,1,0:T(8,128)(2,1)S(1)}, u32[]{:S(2)}, u32[]{:S(2)}) collective-permute-start(bf16[2,3,64,128]{3,2,1,0:T(8,128)(2,1)S(1)} %get-tuple-element.33), channel_id=1, source_target_pairs={{0,4},{4,8},{8,12},{12,16},{16,20},{20,24},{24,28},{1,5},{5,9},{9,... | collective-permute-start | bytes 294920 | tf_op jit(solution)/shard_map/ppermute | solution.py:325
  12.4 6.6 %collective-permute-start.5 = (bf16[13,64,128]{2,1,0:T(8,128)(2,1)S(1)}, bf16[13,64,128]{2,1,0:T(8,128)(2,1)S(1)}, u32[]{:S(2)}, u32[]{:S(2)}) collective-permute-start(bf16[13,64,128]{2,1,0:T(8,128)(2,1)S(1)} %pad_maximum_fusion.refs_4_), channel_id=1, source_target_pairs={{0,2},{1,3},{2,0},{3,1},{4,6},{5,7},{6,4},{7,5},{8,10},{9,11},{10,... | collective-permute-start | bytes 638984 | tf_op jit(solution)/shard_map/ppermute | solution.py:305
  12.7 7.2 %collective-permute-start.1 = (bf16[16,64,128]{2,1,0:T(8,128)(2,1)}, bf16[16,64,128]{2,1,0:T(8,128)(2,1)S(1)}, u32[]{:S(2)}, u32[]{:S(2)}) collective-permute-start(bf16[16,64,128]{2,1,0:T(8,128)(2,1)} %bitcast.12), channel_id=1, source_target_pairs={{0,1},{1,0},{2,3},{3,2},{4,5},{5,4},{6,7},{7,6},{8,9},{9,8},{10,11... | collective-permute-start | bytes 786440 | tf_op jit(solution)/shard_map/ppermute | solution.py:305
  12.7 7.2 %collective-permute-start.2 = (bf16[16,64,128]{2,1,0:T(8,128)(2,1)S(1)}, bf16[16,64,128]{2,1,0:T(8,128)(2,1)S(1)}, u32[]{:S(2)}, u32[]{:S(2)}) collective-permute-start(bf16[16,64,128]{2,1,0:T(8,128)(2,1)S(1)} %collective-permute-done.refs_1_), channel_id=1, source_target_pairs={{0,1},{1,0},{2,3},{3,2},{4,5},{5,4},{6,7},{7,6},{8,9},{9,8},{10,11... | collective-permute-start | bytes 786440 | tf_op jit(solution)/shard_map/ppermute | solution.py:305
  13.2 6.7 %collective-permute-start.6 = (bf16[13,64,128]{2,1,0:T(8,128)(2,1)S(1)}, bf16[13,64,128]{2,1,0:T(8,128)(2,1)S(1)}, u32[]{:S(2)}, u32[]{:S(2)}) collective-permute-start(bf16[13,64,128]{2,1,0:T(8,128)(2,1)S(1)} %pad_maximum_fusion.refs_4_), channel_id=1, source_target_pairs={{0,1},{1,0},{2,3},{3,2},{4,5},{5,4},{6,7},{7,6},{8,9},{9,8},{10,11... | collective-permute-start | bytes 638984 | tf_op jit(solution)/shard_map/ppermute | solution.py:305
  19.0 1.5 %collective-permute-start.7 = (bf16[13,64,128]{2,1,0:T(8,128)(2,1)S(1)}, bf16[13,64,128]{2,1,0:T(8,128)(2,1)S(1)}, u32[]{:S(2)}, u32[]{:S(2)}) collective-permute-start(bf16[13,64,128]{2,1,0:T(8,128)(2,1)S(1)} %collective-permute-done.5.refs_5_), channel_id=1, source_target_pairs={{0,1},{1,0},{2,3},{3,2},{4,5},{5,4},{6,7},{7,6},{8,9},{9,8},{10,11... | collective-permute-start | bytes 638984 | tf_op jit(solution)/shard_map/ppermute | solution.py:305
  19.8 21.0 %copy-start.2 = (s32[2]{0:T(128)S(1)}, s32[2]{0:T(128)}, u32[]{:S(2)}) copy-start(s32[2]{0:T(128)} %charge_ref.7) | copy-start | bytes 28
  20.5 1.0 %copy-start = (bf16[2,8,64,128]{3,2,1,0:T(8,128)(2,1)S(1)}, bf16[2,8,64,128]{3,2,1,0:T(8,128)(2,1)}, u32[]{:S(2)}) copy-start(bf16[2,8,64,128]{3,2,1,0:T(8,128)(2,1)} %param.6) | copy-start | bytes 786436
  21.4 1.0 %copy-start.1 = (bf16[3,3,3,64,64]{4,3,2,1,0:T(8,128)(2,1)S(1)}, bf16[3,3,3,64,64]{4,3,2,1,0:T(8,128)(2,1)}, u32[]{:S(2)}) copy-start(bf16[3,3,3,64,64]{4,3,2,1,0:T(8,128)(2,1)} %filter_ref.1) | copy-start | bytes 663556
  34.6 15.8 %collective-permute-start.8 = (bf16[8,128,128]{2,1,0:T(8,128)(2,1)S(1)}, bf16[8,128,128]{2,1,0:T(8,128)(2,1)S(1)}, u32[]{:S(2)}, u32[]{:S(2)}) collective-permute-start(bf16[8,128,128]{2,1,0:T(8,128)(2,1)S(1)} %get-tuple-element.22.refs_0_), channel_id=1, source_target_pairs={{0,4},{4,8},{8,12},{12,0},{16,20},{20,24},{24,28},{28,16},{1,5},{5... | collective-permute-start | bytes 786440 | tf_op jit(solution)/shard_map/ppermute | solution.py:367
  37.2 13.3 %collective-permute-start.9 = (bf16[8,128,128]{2,1,0:T(8,128)(2,1)S(1)}, bf16[8,128,128]{2,1,0:T(8,128)(2,1)S(1)}, u32[]{:S(2)}, u32[]{:S(2)}) collective-permute-start(bf16[8,128,128]{2,1,0:T(8,128)(2,1)S(1)} %get-tuple-element.22.refs_0_), channel_id=1, source_target_pairs={{0,8},{4,12},{8,0},{12,4},{16,24},{20,28},{24,16},{28,20},{1,9},{5... | collective-permute-start | bytes 786440 | tf_op jit(solution)/shard_map/ppermute | solution.py:367
  38.7 11.7 %collective-permute-start.10 = (bf16[8,128,128]{2,1,0:T(8,128)(2,1)S(1)}, bf16[8,128,128]{2,1,0:T(8,128)(2,1)S(1)}, u32[]{:S(2)}, u32[]{:S(2)}) collective-permute-start(bf16[8,128,128]{2,1,0:T(8,128)(2,1)S(1)} %get-tuple-element.22.refs_0_), channel_id=1, source_target_pairs={{0,12},{4,0},{8,4},{12,8},{16,28},{20,16},{24,20},{28,24},{1,13},{... | collective-permute-start | bytes 786440 | tf_op jit(solution)/shard_map/ppermute | solution.py:367
  51.8 13.6 %collective-permute-start.11 = (bf16[128,128]{1,0:T(8,128)(2,1)S(1)}, bf16[128,128]{1,0:T(8,128)(2,1)S(1)}, u32[]{:S(2)}, u32[]{:S(2)}) collective-permute-start(bf16[128,128]{1,0:T(8,128)(2,1)S(1)} %get-tuple-element.29), channel_id=1, source_target_pairs={{0,16},{4,20},{8,24},{12,28},{16,0},{20,4},{24,8},{28,12},{1,17},{... | collective-permute-start | bytes 98312 | tf_op jit(solution)/shard_map/ppermute | solution.py:395
